TPU v7x, 32 devices: a whole 2x2x4 slice. The times are simulated.
32 devices in a mesh: dp: 16 (over z, y, x), proto: 2 (over core).
Axes of the slice: x: 2, y: 2, z: 4, core: 2. Of those that a mesh axis runs over, the one named last changes fastest.
Arguments:
- teacher: bfloat16 [4096, 128], P('dp'), may hold values from -1000 to 1000
- student: bfloat16 [4096, 128], P('dp'), may hold values from -1000 to 1000
- prototypes: bfloat16 [128, 65536], P('dp', 'proto'), may hold values from -1 to 1, as said below
Outputs:
- crop_loss: float32 [4096], P('dp')
- logit_grad: bfloat16 [4096, 65536], P('dp', 'proto')
- proto_grad: bfloat16 [128, 65536], P('dp', 'proto')
Inputs may be any that keep to these rules, and one draw needn't show every extreme that they name: `prototypes`: prototype columns have unit length.
All inputs are finite; a program needn't handle non-finite values.
Results may differ from a plain program's by a relative error of at most 0.015.
Values may be sent and summed in bfloat16 or wider, within the bound.
No kernel may reach another device: no remote copies, remote signals or barrier semaphores. Data moves between devices by JAX's collectives and lax.ppermute only.
A program may use at most 128 MiB of HBM per device.

v0:
```python
import functools
import math

import jax
import jax.numpy as jnp
from jax import lax
from jax.experimental import pallas as pl
from jax.experimental.pallas import tpu as pltpu
from jax.sharding import PartitionSpec as P

ITERS = 3
F32 = jnp.float32
BF16 = jnp.bfloat16
NT = (((1,), (1,)), ((), ()))
EXTRA = 16
WHOLE = pl.BlockSpec(memory_space=pltpu.VMEM)
FAR = pl.BlockSpec(memory_space=pltpu.HBM)


def params(mib):
    return pltpu.CompilerParams(vmem_limit_bytes=mib * 1024 * 1024)


def cost(flops, nbytes, exps=0):
    return pl.CostEstimate(flops=flops, bytes_accessed=nbytes, transcendentals=exps)


def near(x):
    return pltpu.with_memory_space_constraint(x, pltpu.VMEM)


def far(x):
    return pltpu.with_memory_space_constraint(x, pltpu.HBM)


def full(shape):
    return pl.BlockSpec(shape, lambda i: (0,) * len(shape))


def pieces(v, count):
    out = []
    for _ in range(count):
        p = v.astype(BF16)
        out.append(p)
        v = v - p.astype(F32)
    return out


def rows_of(parts, height):
    n = parts[0].shape[1]
    row = lax.broadcasted_iota(jnp.int32, (height, n), 0)
    block = jnp.zeros((height, n), F32)
    for i, p in enumerate(parts):
        block = jnp.where(row == i, jnp.broadcast_to(p.astype(F32), (height, n)), block)
    return block.astype(BF16)


def exp_kernel(
    rb, kc, resident, protos, crops, x, peak_out, lse_out, protos_t, scores_a, scores_b, *refs
):
    width, n = x.shape
    blocks = n // rb
    for q in range(0, width, 128):
        protos_t[q : q + 128, :] = protos[:, q : q + 128].astype(F32).T.astype(BF16)

    def at(b):
        return pl.ds(b * rb if isinstance(b, int) else pl.multiple_of(b * rb, rb), rb)

    def leave(b, slot):
        return pltpu.make_async_copy(refs[0].at[slot], x.at[:, at(b)], refs[1].at[slot])

    def stage(new, new_scores, old, old_scores, peak, slot=0):
        new_peak = jnp.full((8, rb), -jnp.inf, F32)
        total = jnp.zeros((8, rb), F32)
        for q in range(0, width, kc):
            if new is not None:
                s = lax.dot_general(
                    protos_t[q : q + kc, :], crops[at(new), :], NT, preferred_element_type=F32
                )
                new_scores[q : q + kc, :] = s
                new_peak = jnp.maximum(new_peak, jnp.max(s.reshape(kc // 8, 8, rb), axis=0))
            if old is not None:
                e = jnp.exp(old_scores[q : q + kc, :] - peak)
                total = total + jnp.sum(e.reshape(kc // 8, 8, rb), axis=0)
                if resident:
                    x[q : q + kc, at(old)] = e.astype(BF16)
                else:
                    refs[0][slot, q : q + kc, :] = e.astype(BF16)
        if old is not None:
            peak_out[:, at(old)] = peak
            lse_out[:, at(old)] = peak + jnp.log(jnp.sum(total, axis=0, keepdims=True))
            if not resident:
                leave(old, slot).start()
        return jnp.max(new_peak, axis=0, keepdims=True)

    def free(j, slot):
        if not resident and not (isinstance(j, int) and j == 0):

            @pl.when(j > 0)
            def _():
                leave(2 * j - 2 + slot, slot).wait()

    def two(j, peak):
        free(j, 0)
        peak = stage(2 * j + 1, scores_b, 2 * j, scores_a, peak, 0)
        free(j, 1)
        return stage(2 * j + 2, scores_a, 2 * j + 1, scores_b, peak, 1)

    last = blocks // 2 - 1
    peak = lax.fori_loop(0, last, two, stage(0, scores_a, None, None, None))
    free(last, 0)
    peak = stage(blocks - 1, scores_b, blocks - 2, scores_a, peak, 0)
    free(last, 1)
    stage(None, None, blocks - 1, scores_b, peak, 1)
    if not resident:
        leave(blocks - 2, 0).wait()
        leave(blocks - 1, 1).wait()


def exp_rows(protos, crops, resident):
    depth, width = protos.shape
    n = crops.shape[0]
    rb = 512
    leaving = [pltpu.VMEM((2, width, rb), BF16), pltpu.SemaphoreType.DMA((2,))]
    return pl.pallas_call(
        functools.partial(exp_kernel, rb, 128, resident),
        in_specs=[WHOLE, WHOLE],
        out_specs=[WHOLE if resident else FAR, WHOLE, WHOLE],
        out_shape=[
            (pltpu.VMEM if resident else pltpu.HBM)((width, n), BF16),
            jax.ShapeDtypeStruct((1, n), F32),
            jax.ShapeDtypeStruct((1, n), F32),
        ],
        scratch_shapes=[
            pltpu.VMEM((width, depth), BF16),
            pltpu.VMEM((width, rb), F32),
            pltpu.VMEM((width, rb), F32),
        ]
        + ([] if resident else leaving),
        compiler_params=params(18 if resident else 22),
        cost_estimate=cost(2 * n * width * depth, 2 * n * width, n * width),
        name="exp_rows",
    )(protos, crops)


def sweep_kernel(first, n_all, protos_all, count, x, lead, *refs):
    parts, (part_out, col_out, lead_out, weights, acc) = refs[:count], refs[count:]
    width, n = x.shape
    if first:
        peak = functools.reduce(
            jnp.maximum, [jnp.max(p[...], axis=0, keepdims=True) for p in parts]
        )
        total = sum(jnp.sum(jnp.exp(p[...] - peak), axis=0, keepdims=True) for p in parts)
        lse = peak + jnp.log(total)
        factor = jnp.exp(lead[...] - lse)
        weight = factor
        lead_out[0:1, :] = factor
        lead_out[1:2, :] = lse
    else:
        factor = lead[...]
        total = sum(jnp.sum(p[...], axis=0, keepdims=True) for p in parts)
        weight = factor / (n_all * total)
    weights[...] = jnp.broadcast_to(weight, weights.shape)
    acc[...] = jnp.zeros_like(acc)
    kb = min(512, width)
    row = lax.broadcasted_iota(jnp.int32, (16, kb), 0)

    def scales(q):
        sums = jnp.zeros((kb // 8, 8, 128), F32)
        for r in range(0, n, 128):
            v = x[pl.ds(q, kb), r : r + 128].astype(F32)
            sums = sums + v.reshape(kb // 8, 8, 128) * weights[:, r : r + 128][None]
        sums = sums.reshape(kb, 128)
        sums = [jnp.sum(sums[i : i + 128].T, axis=0, keepdims=True) for i in range(0, kb, 128)]
        return 1.0 / (protos_all * jnp.concatenate(sums, axis=1))

    def totals(q, col):
        col_out[:, pl.ds(q, kb)] = col
        hi = col.astype(BF16).astype(F32)
        rows = jnp.where(row == 0, hi, jnp.where(row == 1, col - hi, 0.0)).astype(BF16)
        acc[...] += jnp.dot(rows, x[pl.ds(q, kb), :], preferred_element_type=F32)

    def both(i, col):
        q = pl.multiple_of(i * kb, kb)
        later = scales(pl.multiple_of(q + kb, kb))
        totals(q, col)
        return later

    totals(width - kb, lax.fori_loop(0, width // kb - 1, both, scales(0)))
    part_out[...] = jnp.sum(acc[...], axis=0, keepdims=True) * factor


def sweep(first, n_all, protos_all, x, lead, parts):
    width, n = x.shape
    return pl.pallas_call(
        functools.partial(sweep_kernel, first, float(n_all), float(protos_all), len(parts)),
        in_specs=[WHOLE] * (2 + len(parts)),
        out_specs=[WHOLE] * 3,
        out_shape=[
            jax.ShapeDtypeStruct((1, n), F32),
            jax.ShapeDtypeStruct((1, width), F32),
            jax.ShapeDtypeStruct((2, n), F32),
        ],
        scratch_shapes=[pltpu.VMEM((8, n), F32), pltpu.VMEM((16, n), F32)],
        compiler_params=params(8),
        cost_estimate=cost(4 * n * width, 2 * n * width),
        name="sweep",
    )(near(x), lead, *parts)


def weighted_student(weight, student, weighted):
    n, depth = student.shape
    for r in range(0, n, 128):
        s = student[r : r + 128, :].astype(F32).T * weight[:, r : r + 128]
        hi, lo = pieces(s, 2)
        weighted[:depth, r : r + 128] = hi
        weighted[depth:, r : r + 128] = lo


def soft_kernel(x, peak, lse, student, out, weighted):
    depth = student.shape[1]

    @pl.when(pl.program_id(0) == 0)
    def _():
        weighted_student(jnp.exp(peak[...] - lse[...]), student, weighted)

    g = lax.dot_general(x[...], weighted[...], NT, preferred_element_type=F32)
    out[...] = g[:, :depth] + g[:, depth:]


def soft_part(x, peak, lse, student):
    width, n = x.shape
    depth = student.shape[1]
    kb = min(512, width)
    return pl.pallas_call(
        soft_kernel,
        grid=(width // kb,),
        in_specs=[
            pl.BlockSpec((kb, n), lambda i: (i, 0)),
            full((1, n)),
            full((1, n)),
            full((n, depth)),
        ],
        out_specs=pl.BlockSpec((kb, depth), lambda i: (i, 0)),
        out_shape=jax.ShapeDtypeStruct((width, depth), F32),
        scratch_shapes=[pltpu.VMEM((2 * depth, n), BF16)],
        compiler_params=params(24),
        cost_estimate=cost(2 * n * width * depth, 2 * n * width),
        name="soft_part",
    )(far(x), peak, lse, student)


def grad_kernel(scale, x, factor, student, soft, col, *refs):
    ends, (out, weighted) = refs[:-2], refs[-2:]
    width = x.shape[0]
    depth = student.shape[1]
    n = x.shape[1]
    total = sum(e[:, :n] for e in ends)
    weighted_student(factor[...] / total, student, weighted)
    g = lax.dot_general(x[...], weighted[...], NT, preferred_element_type=F32)
    g = g[:, :depth] + g[:, depth:]
    for k in range(0, width, 128):
        a = soft[k : k + 128, :].T
        b = g[k : k + 128, :].T
        out[:, k : k + 128] = (scale * (a - b * col[:, k : k + 128])).astype(BF16)


def proto_grad_columns(scale, x, factor, student, soft, col, ends):
    width, n = x.shape
    depth = student.shape[1]
    return pl.pallas_call(
        functools.partial(grad_kernel, scale),
        in_specs=[WHOLE] * (5 + len(ends)),
        out_specs=WHOLE,
        out_shape=jax.ShapeDtypeStruct((depth, width), BF16),
        scratch_shapes=[pltpu.VMEM((2 * depth, n), BF16)],
        compiler_params=params(18),
        cost_estimate=cost(2 * n * width * depth, 2 * n * width),
        name="proto_grad",
    )(near(x), factor, student, soft, col, *ends)


def logit_kernel(protos_all, share, chunk, protos, teacher, student, glob_t, glob_s, *refs):
    ends = refs[:-8]
    grad_out, loss_out, lhs, rhs, grads, loss, in_sem, out_sem = refs[-8:]
    n = glob_t.shape[1]
    slots, rows, cb = grads.shape
    depth, width = protos.shape
    steps = width // cb

    def fetch(c):
        at = pl.ds(c * cb, cb)
        return pltpu.make_async_copy(protos.at[:, at], rhs.at[:depth, at], in_sem.at[c])

    def store(c, slot):
        at = pl.ds(pl.multiple_of(c * cb, cb), cb)
        return pltpu.make_async_copy(grads.at[slot], grad_out.at[:, at], out_sem.at[slot])

    for c in range(steps):
        fetch(c).start()

    lhs[:rows, :depth] = teacher[...]
    lhs[rows:, :depth] = student[...]
    me = lax.axis_index("dp")
    here = pl.ds(pl.multiple_of(me * rows, rows), rows)
    biases = (
        -jnp.log(sum(e[:, here] for e in ends)) - glob_t[:, here],
        math.log(protos_all) - glob_s[:, here],
    )
    lane = lax.broadcasted_iota(jnp.int32, (rows, 128), 1)
    for i, bias in enumerate(biases):
        b = jnp.broadcast_to(bias, (128, rows)).T
        ext = jnp.zeros((rows, 128), F32)
        for j, p in enumerate(pieces(b, 3)):
            ext = jnp.where(lane == j, p.astype(F32), ext)
        if i == 0:
            ext = jnp.where((lane >= 3) & (lane < 6), 1.0, ext)
        lhs[i * rows : (i + 1) * rows, depth:] = ext.astype(BF16)[:, :EXTRA]
    one = jnp.ones((1, share), F32)
    for d in range(width // share):
        e, j = divmod(d, len(ends))
        log_col = jnp.log(protos_all * ends[j][:, n + e * share : n + (e + 1) * share])
        to = pl.ds(pl.multiple_of((d ^ me) * share, share), share)
        rhs[depth:, to] = rows_of([one] * 3 + pieces(log_col, 3), EXTRA)
    loss[...] = jnp.zeros_like(loss)

    @pl.loop(0, steps)
    def _(c):
        slot = lax.rem(c, slots)

        @pl.when(c >= slots)
        def _():
            store(c - slots, slot).wait()

        pltpu.make_async_copy(
            protos.at[:, pl.ds(0, cb)], rhs.at[:depth, pl.ds(0, cb)], in_sem.at[c]
        ).wait()
        half = rows // 2
        for k in range(0, cb, chunk):
            at = pl.ds(pl.multiple_of(c * cb + k, chunk), chunk)
            for r in (0, half):
                here = slice(r, r + half)
                t = jnp.exp(jnp.dot(lhs[here, :], rhs[:, at], preferred_element_type=F32))
                u = jnp.dot(
                    lhs[rows + r : rows + r + half, :], rhs[:, at], preferred_element_type=F32
                )
                grads[slot, here, k : k + chunk] = (jnp.exp(u) - t).astype(BF16)
                p = t * u
                loss[here, :] += sum(p[:, j : j + 128] for j in range(0, chunk, 128))
        store(c, slot).start()

    for c in range(max(0, steps - slots), steps):
        store(c, c % slots).wait()
    loss_out[...] = jnp.sum(loss[...].T, axis=0, keepdims=True)


def logit_grads(protos_all, share, protos, teacher, student, glob_t, glob_s, ends):
    depth, width = protos.shape
    rows = teacher.shape[0]
    cb = min(4096, width)
    slots = min(4, width // cb)
    return pl.pallas_call(
        functools.partial(logit_kernel, float(protos_all), share, min(256, cb)),
        in_specs=[FAR] + [WHOLE] * (4 + len(ends)),
        out_specs=[FAR, WHOLE],
        out_shape=[
            pltpu.HBM((rows, width), BF16),
            jax.ShapeDtypeStruct((1, rows), F32),
        ],
        scratch_shapes=[
            pltpu.VMEM((2 * rows, depth + EXTRA), BF16),
            pltpu.VMEM((depth + EXTRA, width), BF16),
            pltpu.VMEM((slots, rows, cb), BF16),
            pltpu.VMEM((rows, 128), F32),
            pltpu.SemaphoreType.DMA((width // cb,)),
            pltpu.SemaphoreType.DMA((slots,)),
        ],
        compiler_params=params(58),
        cost_estimate=cost(
            4 * rows * width * depth, 2 * width * (rows + depth), 2 * rows * width
        ),
        name="logit_grads",
    )(far(protos), teacher, student, glob_t, glob_s, *ends)


def over_proto(v, combine):
    size = lax.axis_size("proto")
    if size == 2:
        return combine([v, lax.ppermute(v, "proto", [(0, 1), (1, 0)])])
    got = lax.all_gather(v, "proto")
    return combine([got[i] for i in range(size)])


def add(parts):
    return functools.reduce(jnp.add, parts)


def log_add(parts):
    peak = functools.reduce(jnp.maximum, parts)
    return peak + jnp.log(sum(jnp.exp(p - peak) for p in parts))


def dp_rounds():
    size = lax.axis_size("dp")
    rounds, bit = [], 1
    while bit < size:
        step = min(4, size // bit)
        rounds.append([s * bit for s in range(1, step)])
        bit *= step
    return rounds[::-1]


def swap(v, mask):
    size = lax.axis_size("dp")
    return lax.ppermute(v, "dp", [(a, a ^ mask) for a in range(size)])


def from_partners(v, masks):
    return [v] + [swap(v, m) for m in masks]


def radix4(v, combine, fill=None, args=()):
    rounds = dp_rounds()
    out = None
    if fill is not None:
        v, args = lax.optimization_barrier((v, args))
    for i, masks in enumerate(rounds):
        got = from_partners(v, masks)
        if i == 0 and fill is not None:
            got, out = lax.optimization_barrier((got, fill(*args)))
        if i == len(rounds) - 1:
            return got, out
        v = combine(got)


def in_dp_order(v):
    rest = v.shape[1:]
    size = lax.axis_size("dp")
    me = lax.axis_index("dp")
    bit = 1
    while bit < size:
        w = v.reshape((size // (2 * bit), 2, bit) + rest)
        w = jnp.where((me & bit) != 0, w[:, ::-1], w)
        v = w.reshape((size,) + rest)
        bit *= 2
    return v


def gather_round(v, masks):
    return jnp.stack(from_partners(v, masks), axis=1).reshape((-1,) + v.shape[1:])


def own_share(v):
    size = lax.axis_size("proto")
    rows = v.shape[0] // size
    return lax.dynamic_slice_in_dim(v, lax.axis_index("proto") * rows, rows, 0)


def both_shares(v):
    size = lax.axis_size("proto")
    if size == 2:
        other = lax.ppermute(v, "proto", [(0, 1), (1, 0)])
        mine = lax.axis_index("proto") == 0
        return jnp.concatenate([jnp.where(mine, v, other), jnp.where(mine, other, v)], axis=1)
    return lax.all_gather(v, "proto", axis=1, tiled=True)


def shards(teacher, student, prototypes):
    rows, depth = teacher.shape
    dp = lax.axis_size("dp")
    n = rows * dp
    protos_all = prototypes.shape[1] * lax.axis_size("proto")
    width = prototypes.shape[1] // dp

    own = lax.all_to_all(prototypes, "dp", 1, 0, tiled=True)
    crops = jnp.stack([own_share(teacher), own_share(student)])[None]
    rounds = dp_rounds()
    for masks in rounds[:-1]:
        crops = gather_round(crops, masks)
    own, crops, prototypes = lax.optimization_barrier((own, crops, prototypes))
    gathered = lax.all_gather(prototypes, "dp", axis=0, tiled=True)
    teacher_all, student_all = [
        both_shares(in_dp_order(gather_round(crops[:, i], rounds[-1]))).reshape(n, depth)
        for i in range(2)
    ]

    x_t, peak_t, lse_t = exp_rows(own, teacher_all, True)
    lses, (x_s, peak_s, lse_s) = radix4(
        over_proto(lse_t, log_add),
        log_add,
        lambda crops: exp_rows(own, crops, False),
        (student_all,),
    )
    part, col, lead = sweep(True, n, protos_all, x_t, peak_t, lses)
    factor, glob_t = lead[:1], lead[1:]

    def mixed(parts):
        return jnp.concatenate([add([p[:1] for p in parts]), log_add([p[1:] for p in parts])])

    soft = None
    for it in range(1, ITERS):
        part = over_proto(part, add)
        if it == 1:
            got, _ = radix4(jnp.concatenate([part, over_proto(lse_s, log_add)]), mixed)
            glob_s = log_add([p[1:] for p in got])
            got = [p[:1] for p in got]
        else:
            got, soft = radix4(
                part,
                add,
                lambda peak: soft_part(x_s, peak, glob_s, student_all),
                (peak_s,),
            )
        part, col, _ = sweep(False, n, protos_all, x_t, factor, got)

    ends = [jnp.concatenate([over_proto(part, add), col], axis=1)]
    for masks in dp_rounds():
        if len(ends) > 1:
            total = add([e[:, :n] for e in ends])
            cols = jnp.stack([e[:, n:].reshape(-1, width) for e in ends], axis=1)
            ends = [jnp.concatenate([total, cols.reshape(1, -1)], axis=1)]
        ends = from_partners(ends[0], masks)

    grad = proto_grad_columns(protos_all / 128.0, x_t, factor, student_all, soft, col, ends)
    proto_grad = lax.all_to_all(grad, "dp", 0, 1, tiled=True)

    logit_grad, loss = logit_grads(
        protos_all, width, gathered, teacher, student, glob_t, glob_s, ends
    )
    crop_loss = math.log(protos_all) - over_proto(loss[0], add) / protos_all
    return crop_loss, logit_grad, proto_grad


def solution(mesh):
    placed = (P("dp", None), P("dp", None), P("dp", "proto"))
    return jax.shard_map(
        shards,
        mesh=mesh,
        in_specs=placed,
        out_specs=(P("dp"), P("dp", "proto"), P("dp", "proto")),
        check_vma=False,
    )
```

profile of v0, /device:TPU:0, one launch (start us, length us, event | category | flops | bytes accessed | tf_op | source)
XLA Modules:
  0.0 194.9 jit_solution(1350485296143174500)
XLA Ops:
  7.2 8.3 %all-to-all-start = ((bf16[8,16,2048]{2,0,1:T(8,128)(2,1)}), bf16[8,16,2048]{2,0,1:T(8,128)(2,1)S(1)}, u32[]{:S(2)}, u32[]{:S(2)}) async-start(bf16[8,16,2048]{2,0,1:T(8,128)(2,1)} %bitcast.79), calls=%async_computation | async-start | bytes 1048576 | tf_op jit(solution)/shard_map/all_to_all | solution.py:475
  16.3 2.0 %collective-permute-start = (bf16[1,2,128,128]{3,2,1,0:T(8,128)(2,1)S(1)}, bf16[1,2,128,128]{3,2,1,0:T(8,128)(2,1)S(1)}, u32[]{:S(2)}, u32[]{:S(2)}) collective-permute-start(bf16[1,2,128,128]{3,2,1,0:T(8,128)(2,1)S(1)} %get-tuple-element.78), channel_id=1, source_target_pairs={{0,8},{2,10},{4,12},{6,14},{8,0},{10,2},{12,4},{14,6},{16,24},{18,... | collective-permute-start | bytes 196616 | tf_op jit(solution)/shard_map/ppermute | solution.py:415
  18.3 2.4 %collective-permute-start.1 = (bf16[1,2,128,128]{3,2,1,0:T(8,128)(2,1)S(1)}, bf16[1,2,128,128]{3,2,1,0:T(8,128)(2,1)S(1)}, u32[]{:S(2)}, u32[]{:S(2)}) collective-permute-start(bf16[1,2,128,128]{3,2,1,0:T(8,128)(2,1)S(1)} %get-tuple-element.78), channel_id=1, source_target_pairs={{0,16},{2,18},{4,20},{6,22},{8,24},{10,26},{12,28},{14,30},{16,0},... | collective-permute-start | bytes 196616 | tf_op jit(solution)/shard_map/ppermute | solution.py:415
  20.8 6.1 %collective-permute-done = bf16[1,2,128,128]{3,2,1,0:T(8,128)(2,1)S(1)} collective-permute-done((bf16[1,2,128,128]{3,2,1,0:T(8,128)(2,1)S(1)}, bf16[1,2,128,128]{3,2,1,0:T(8,128)(2,1)S(1)}, u32[]{:S(2)}, u32[]{:S(2)}) %collective-permute-start) | collective-permute-done | bytes 65568 | tf_op jit(solution)/shard_map/ppermute | solution.py:415
  26.9 7.9 %collective-permute-done.1 = bf16[1,2,128,128]{3,2,1,0:T(8,128)(2,1)S(1)} collective-permute-done((bf16[1,2,128,128]{3,2,1,0:T(8,128)(2,1)S(1)}, bf16[1,2,128,128]{3,2,1,0:T(8,128)(2,1)S(1)}, u32[]{:S(2)}, u32[]{:S(2)}) %collective-permute-start.1) | collective-permute-done | bytes 65568 | tf_op jit(solution)/shard_map/ppermute | solution.py:415
  41.5 2.3 %collective-permute-start.10 = (bf16[4,128,128]{2,1,0:T(8,128)(2,1)S(1)}, bf16[4,128,128]{2,1,0:T(8,128)(2,1)S(1)}, u32[]{:S(2)}, u32[]{:S(2)}) collective-permute-start(bf16[4,128,128]{2,1,0:T(8,128)(2,1)S(1)} %get-tuple-element.73), channel_id=1, source_target_pairs={{0,6},{2,4},{4,2},{6,0},{8,14},{10,12},{12,10},{14,8},{16,22},{18,... | collective-permute-start | bytes 393224 | tf_op jit(solution)/shard_map/ppermute | solution.py:415
  49.7 10.0 %exp_rows.2 = (bf16[2048,4096]{1,0:T(8,128)(2,1)S(1)}, f32[1,4096]{1,0:T(1,128)S(1)}, f32[1,4096]{1,0:T(1,128)S(1)}) custom-call(bf16[128,2048]{1,0:T(8,128)(2,1)S(1)} %bitcast.74, bf16[4096,128]{1,0:T(8,128)(2,1)S(1)} %bitcast.73), custom_call_target="tpu_custom_call" | custom-call | flops 2147483648 | bytes 16777216 | tf_op jit(solution)/shard_map/exp_rows/pallas_call | solution.py:125
  61.2 2.2 %collective-permute-start.12 = (f32[1,4096]{1,0:T(1,128)S(1)}, f32[1,4096]{1,0:T(1,128)S(1)}, u32[]{:S(2)}, u32[]{:S(2)}) collective-permute-start(f32[1,4096]{1,0:T(1,128)S(1)} %log_add_fusion.4), channel_id=1, source_target_pairs={{0,8},{2,10},{4,12},{6,14},{8,0},{10,2},{12,4},{14,6},{16,24},{18,... | collective-permute-start | bytes 49160 | tf_op jit(solution)/shard_map/ppermute | solution.py:415
  65.9 11.9 %exp_rows.3 = (bf16[2048,4096]{1,0:T(8,128)(2,1)}, f32[1,4096]{1,0:T(1,128)S(1)}, f32[1,4096]{1,0:T(1,128)S(1)}) custom-call(bf16[128,2048]{1,0:T(8,128)(2,1)S(1)} %bitcast.75, bf16[4096,128]{1,0:T(8,128)(2,1)S(1)} %bitcast.70), custom_call_target="tpu_custom_call" | custom-call | flops 2147483648 | bytes 16777216 | tf_op jit(solution)/shard_map/exp_rows/pallas_call | solution.py:125
  82.4 2.0 %collective-permute-done.17.refs_3_ = f32[1,4096]{1,0:T(1,128)S(1)} collective-permute-done((f32[1,4096]{1,0:T(1,128)S(1)}, f32[1,4096]{1,0:T(1,128)S(1)}, u32[]{:S(2)}, u32[]{:S(2)}) %collective-permute-start.17) | collective-permute-done | bytes 16416 | tf_op jit(solution)/shard_map/ppermute | solution.py:415
  84.5 6.4 %sweep.3 = (f32[1,4096]{1,0:T(1,128)S(1)}, f32[1,2048]{1,0:T(1,128)}, f32[2,4096]{1,0:T(2,128)S(1)}) custom-call(bf16[2048,4096]{1,0:T(8,128)(2,1)S(1)} %get-tuple-element.38.x, f32[1,4096]{1,0:T(1,128)S(1)} %get-tuple-element.39.lead, f32[1,4096]{1,0:T(1,128)S(1)} %log_add_fusion.3.refs_0_, f32[1,4096]{1,0:T(1,128)S(1)} %collective-permute-done.15.refs_1_, ...), custom_call_target="tpu_custom_call" | custom-call | flops 33554432 | bytes 16777216 | tf_op jit(solution)/shard_map/sweep/pallas_call | solution.py:195
  97.0 2.3 %collective-permute-done.21 = f32[2,4096]{1,0:T(2,128)S(1)} collective-permute-done((f32[2,4096]{1,0:T(2,128)S(1)}, f32[2,4096]{1,0:T(2,128)S(1)}, u32[]{:S(2)}, u32[]{:S(2)}) %collective-permute-start.21) | collective-permute-done | bytes 32800 | tf_op jit(solution)/shard_map/ppermute | solution.py:415
  106.5 2.4 %collective-permute-done.25 = f32[2,4096]{1,0:T(2,128)S(1)} collective-permute-done((f32[2,4096]{1,0:T(2,128)S(1)}, f32[2,4096]{1,0:T(2,128)S(1)}, u32[]{:S(2)}, u32[]{:S(2)}) %collective-permute-start.25) | collective-permute-done | bytes 32800 | tf_op jit(solution)/shard_map/ppermute | solution.py:415
  109.0 6.2 %sweep.4 = (f32[1,4096]{1,0:T(1,128)S(1)}, f32[1,2048]{1,0:T(1,128)}, f32[2,4096]{1,0:T(2,128)}) custom-call(bf16[2048,4096]{1,0:T(8,128)(2,1)S(1)} %get-tuple-element.38.x, f32[1,4096]{1,0:T(1,128)S(1)} %get-tuple-element.83.lead.factor, f32[1,4096]{1,0:T(1,128)S(1)} %get-tuple-element.75.refs_0_, f32[1,4096]{1,0:T(1,128)S(1)} %get-tuple-element.82.refs_1_, ...), custom_call_target="tpu_custom_call" | custom-call | flops 33554432 | bytes 16777216 | tf_op jit(solution)/shard_map/sweep/pallas_call | solution.py:195
  116.5 2.0 %collective-permute-start.28 = (f32[1,4096]{1,0:T(1,128)S(1)}, f32[1,4096]{1,0:T(1,128)S(1)}, u32[]{:S(2)}, u32[]{:S(2)}) collective-permute-start(f32[1,4096]{1,0:T(1,128)S(1)} %add.112), channel_id=1, source_target_pairs={{0,16},{2,18},{4,20},{6,22},{8,24},{10,26},{12,28},{14,30},{16,0},... | collective-permute-start | bytes 49160 | tf_op jit(solution)/shard_map/ppermute | solution.py:415
  118.5 2.4 %collective-permute-start.29 = (f32[1,4096]{1,0:T(1,128)S(1)}, f32[1,4096]{1,0:T(1,128)S(1)}, u32[]{:S(2)}, u32[]{:S(2)}) collective-permute-start(f32[1,4096]{1,0:T(1,128)S(1)} %add.112), channel_id=1, source_target_pairs={{0,24},{2,26},{4,28},{6,30},{8,16},{10,18},{12,20},{14,22},{16,8},... | collective-permute-start | bytes 49160 | tf_op jit(solution)/shard_map/ppermute | solution.py:415
  120.9 9.1 %soft_part.1.soft = f32[2048,128]{1,0:T(8,128)S(1)} custom-call(bf16[2048,4096]{1,0:T(8,128)(2,1)} %get-tuple-element.56.x, f32[1,4096]{1,0:T(1,128)S(1)} %get-tuple-element.57.peak, f32[1,4096]{1,0:T(1,128)S(1)} %get-tuple-element.80.lse.glob_s, bf16[4096,128]{1,0:T(8,128)(2,1)S(1)} %bitcast.71), custom_call_target="tpu_custom_call" | custom-call | flops 2147483648 | bytes 16777216 | tf_op jit(solution)/shard_map/soft_part/pallas_call | solution.py:235
  131.3 2.3 %collective-permute-start.32 = (f32[1,4096]{1,0:T(1,128)S(1)}, f32[1,4096]{1,0:T(1,128)S(1)}, u32[]{:S(2)}, u32[]{:S(2)}) collective-permute-start(f32[1,4096]{1,0:T(1,128)S(1)} %add_add_fusion.refs_0_), channel_id=1, source_target_pairs={{0,6},{2,4},{4,2},{6,0},{8,14},{10,12},{12,10},{14,8},{16,22},{18,... | collective-permute-start | bytes 49160 | tf_op jit(solution)/shard_map/ppermute | solution.py:415
  136.3 6.4 %sweep.5 = (f32[1,4096]{1,0:T(1,128)S(1)}, f32[1,2048]{1,0:T(1,128)S(1)}, f32[2,4096]{1,0:T(2,128)}) custom-call(bf16[2048,4096]{1,0:T(8,128)(2,1)S(1)} %get-tuple-element.38.x, f32[1,4096]{1,0:T(1,128)S(1)} %get-tuple-element.83.lead.factor, f32[1,4096]{1,0:T(1,128)S(1)} %add_add_fusion.refs_0_, f32[1,4096]{1,0:T(1,128)S(1)} %collective-permute-done.30.refs_1_, ...), custom_call_target="tpu_custom_call" | custom-call | flops 33554432 | bytes 16777216 | tf_op jit(solution)/shard_map/sweep/pallas_call | solution.py:195
  145.6 2.8 %collective-permute-start.35 = (f32[1,6144]{1,0:T(1,128)S(1)}, f32[1,6144]{1,0:T(1,128)S(1)}, u32[]{:S(2)}, u32[]{:S(2)}) collective-permute-start(f32[1,6144]{1,0:T(1,128)S(1)} %pad_maximum_fusion.8), channel_id=1, source_target_pairs={{0,16},{2,18},{4,20},{6,22},{8,24},{10,26},{12,28},{14,30},{16,0},... | collective-permute-start | bytes 73736 | tf_op jit(solution)/shard_map/ppermute | solution.py:415
  148.4 2.0 %collective-permute-done.36 = f32[1,6144]{1,0:T(1,128)S(1)} collective-permute-done((f32[1,6144]{1,0:T(1,128)S(1)}, f32[1,6144]{1,0:T(1,128)S(1)}, u32[]{:S(2)}, u32[]{:S(2)}) %collective-permute-start.36) | collective-permute-done | bytes 24608 | tf_op jit(solution)/shard_map/ppermute | solution.py:415
  159.4 5.8 %proto_grad.1 = bf16[128,2048]{1,0:T(8,128)(2,1)} custom-call(bf16[2048,4096]{1,0:T(8,128)(2,1)S(1)} %get-tuple-element.38.x, f32[1,4096]{1,0:T(1,128)S(1)} %get-tuple-element.83.lead.factor, bf16[4096,128]{1,0:T(8,128)(2,1)S(1)} %bitcast.72, f32[2048,128]{1,0:T(8,128)S(1)} %soft_part.1.soft, f32[1,2048]{1,0:T(1,128)S(1)} %get-tuple-element.63.col, ...), custom_call_target="tpu_custom_call" | custom-call | flops 2147483648 | bytes 16777216 | tf_op jit(solution)/shard_map/proto_grad/pallas_call | solution.py:271
  165.2 4.5 %all-to-all-start.1 = ((bf16[16,8,2048]{2,1,0:T(8,128)(2,1)}), bf16[16,8,2048]{2,1,0:T(8,128)(2,1)S(1)}, u32[]{:S(2)}, u32[]{:S(2)}) async-start(bf16[16,8,2048]{2,1,0:T(8,128)(2,1)} %bitcast.42), calls=%async_computation.1 | async-start | bytes 1048576 | tf_op jit(solution)/shard_map/all_to_all | solution.py:525
  169.7 14.8 %logit_grads.1 = (bf16[256,32768]{1,0:T(8,128)(2,1)}, f32[1,256]{1,0:T(1,128)}) custom-call(bf16[128,32768]{1,0:T(8,128)(2,1)} %all-gather.2.cloned.1.call-done.protos, bf16[256,128]{1,0:T(8,128)(2,1)} %teacher.1, bf16[256,128]{1,0:T(8,128)(2,1)} %student.1, f32[1,4096]{1,0:T(1,128)} %get-tuple-element.84.glob_t, f32[1,4096]{1,0:T(1,128)} %copy-done.1, ...), custom_call_target="tpu_custom_call" | custom-call | flops 4294967296 | bytes 25165824 | tf_op jit(solution)/shard_map/logit_grads/pallas_call | solution.py:362
  (123 shorter events, 56.0 us)
Async XLA Ops:
  7.2 27.7 %all-to-all-start = ((bf16[8,16,2048]{2,0,1:T(8,128)(2,1)}), bf16[8,16,2048]{2,0,1:T(8,128)(2,1)S(1)}, u32[]{:S(2)}, u32[]{:S(2)}) async-start(bf16[8,16,2048]{2,0,1:T(8,128)(2,1)} %bitcast.79), calls=%async_computation | async-start | bytes 1048576 | tf_op jit(solution)/shard_map/all_to_all | solution.py:475
  15.5 154.2 %all-gather.2.cloned.1.call-start = ((), (), s32[]{:S(2)}) async-start(), calls=%async_computation.2 | async-start | bytes 8912896 | tf_op jit(solution)/shard_map/all_gather | solution.py:481
  16.3 10.5 %collective-permute-start = (bf16[1,2,128,128]{3,2,1,0:T(8,128)(2,1)S(1)}, bf16[1,2,128,128]{3,2,1,0:T(8,128)(2,1)S(1)}, u32[]{:S(2)}, u32[]{:S(2)}) collective-permute-start(bf16[1,2,128,128]{3,2,1,0:T(8,128)(2,1)S(1)} %get-tuple-element.78), channel_id=1, source_target_pairs={{0,8},{2,10},{4,12},{6,14},{8,0},{10,2},{12,4},{14,6},{16,24},{18,... | collective-permute-start | bytes 196616 | tf_op jit(solution)/shard_map/ppermute | solution.py:415
  18.3 16.5 %collective-permute-start.1 = (bf16[1,2,128,128]{3,2,1,0:T(8,128)(2,1)S(1)}, bf16[1,2,128,128]{3,2,1,0:T(8,128)(2,1)S(1)}, u32[]{:S(2)}, u32[]{:S(2)}) collective-permute-start(bf16[1,2,128,128]{3,2,1,0:T(8,128)(2,1)S(1)} %get-tuple-element.78), channel_id=1, source_target_pairs={{0,16},{2,18},{4,20},{6,22},{8,24},{10,26},{12,28},{14,30},{16,0},... | collective-permute-start | bytes 196616 | tf_op jit(solution)/shard_map/ppermute | solution.py:415
  20.7 14.1 %collective-permute-start.2 = (bf16[1,2,128,128]{3,2,1,0:T(8,128)(2,1)S(1)}, bf16[1,2,128,128]{3,2,1,0:T(8,128)(2,1)S(1)}, u32[]{:S(2)}, u32[]{:S(2)}) collective-permute-start(bf16[1,2,128,128]{3,2,1,0:T(8,128)(2,1)S(1)} %get-tuple-element.78), channel_id=1, source_target_pairs={{0,24},{2,26},{4,28},{6,30},{8,16},{10,18},{12,20},{14,22},{16,8},... | collective-permute-start | bytes 196616 | tf_op jit(solution)/shard_map/ppermute | solution.py:415
  35.0 6.5 %collective-permute-start.3 = (bf16[4,128,128]{2,1,0:T(8,128)(2,1)S(1)}, bf16[4,128,128]{2,1,0:T(8,128)(2,1)S(1)}, u32[]{:S(2)}, u32[]{:S(2)}) collective-permute-start(bf16[4,128,128]{2,1,0:T(8,128)(2,1)S(1)} %get-tuple-element.72), channel_id=1, source_target_pairs={{0,2},{2,0},{4,6},{6,4},{8,10},{10,8},{12,14},{14,12},{16,18},{18,... | collective-permute-start | bytes 393224 | tf_op jit(solution)/shard_map/ppermute | solution.py:415
  36.5 7.7 %collective-permute-start.4 = (bf16[4,128,128]{2,1,0:T(8,128)(2,1)S(1)}, bf16[4,128,128]{2,1,0:T(8,128)(2,1)S(1)}, u32[]{:S(2)}, u32[]{:S(2)}) collective-permute-start(bf16[4,128,128]{2,1,0:T(8,128)(2,1)S(1)} %get-tuple-element.72), channel_id=1, source_target_pairs={{0,4},{2,6},{4,0},{6,2},{8,12},{10,14},{12,8},{14,10},{16,20},{18,... | collective-permute-start | bytes 393224 | tf_op jit(solution)/shard_map/ppermute | solution.py:415
  38.0 7.4 %collective-permute-start.5 = (bf16[4,128,128]{2,1,0:T(8,128)(2,1)S(1)}, bf16[4,128,128]{2,1,0:T(8,128)(2,1)S(1)}, u32[]{:S(2)}, u32[]{:S(2)}) collective-permute-start(bf16[4,128,128]{2,1,0:T(8,128)(2,1)S(1)} %get-tuple-element.72), channel_id=1, source_target_pairs={{0,6},{2,4},{4,2},{6,0},{8,14},{10,12},{12,10},{14,8},{16,22},{18,... | collective-permute-start | bytes 393224 | tf_op jit(solution)/shard_map/ppermute | solution.py:415
  38.5 8.0 %collective-permute-start.8 = (bf16[4,128,128]{2,1,0:T(8,128)(2,1)S(1)}, bf16[4,128,128]{2,1,0:T(8,128)(2,1)S(1)}, u32[]{:S(2)}, u32[]{:S(2)}) collective-permute-start(bf16[4,128,128]{2,1,0:T(8,128)(2,1)S(1)} %get-tuple-element.73), channel_id=1, source_target_pairs={{0,2},{2,0},{4,6},{6,4},{8,10},{10,8},{12,14},{14,12},{16,18},{18,... | collective-permute-start | bytes 393224 | tf_op jit(solution)/shard_map/ppermute | solution.py:415
  40.0 7.4 %collective-permute-start.9 = (bf16[4,128,128]{2,1,0:T(8,128)(2,1)S(1)}, bf16[4,128,128]{2,1,0:T(8,128)(2,1)S(1)}, u32[]{:S(2)}, u32[]{:S(2)}) collective-permute-start(bf16[4,128,128]{2,1,0:T(8,128)(2,1)S(1)} %get-tuple-element.73), channel_id=1, source_target_pairs={{0,4},{2,6},{4,0},{6,2},{8,12},{10,14},{12,8},{14,10},{16,20},{18,... | collective-permute-start | bytes 393224 | tf_op jit(solution)/shard_map/ppermute | solution.py:415
  41.5 7.3 %collective-permute-start.10 = (bf16[4,128,128]{2,1,0:T(8,128)(2,1)S(1)}, bf16[4,128,128]{2,1,0:T(8,128)(2,1)S(1)}, u32[]{:S(2)}, u32[]{:S(2)}) collective-permute-start(bf16[4,128,128]{2,1,0:T(8,128)(2,1)S(1)} %get-tuple-element.73), channel_id=1, source_target_pairs={{0,6},{2,4},{4,2},{6,0},{8,14},{10,12},{12,10},{14,8},{16,22},{18,... | collective-permute-start | bytes 393224 | tf_op jit(solution)/shard_map/ppermute | solution.py:415
  49.4 10.9 %collective-permute-start.11 = (bf16[16,128,128]{2,1,0:T(8,128)(2,1)S(1)}, bf16[16,128,128]{2,1,0:T(8,128)(2,1)S(1)}, u32[]{:S(2)}, u32[]{:S(2)}) collective-permute-start(bf16[16,128,128]{2,1,0:T(8,128)(2,1)S(1)} %bitcast.78), channel_id=1, source_target_pairs={{0,1},{1,0},{2,3},{3,2},{4,5},{5,4},{6,7},{7,6},{8,9},{9,8},{10,11... | collective-permute-start | bytes 1572872 | tf_op jit(solution)/shard_map/ppermute | solution.py:462
  61.2 16.6 %collective-permute-start.12 = (f32[1,4096]{1,0:T(1,128)S(1)}, f32[1,4096]{1,0:T(1,128)S(1)}, u32[]{:S(2)}, u32[]{:S(2)}) collective-permute-start(f32[1,4096]{1,0:T(1,128)S(1)} %log_add_fusion.4), channel_id=1, source_target_pairs={{0,8},{2,10},{4,12},{6,14},{8,0},{10,2},{12,4},{14,6},{16,24},{18,... | collective-permute-start | bytes 49160 | tf_op jit(solution)/shard_map/ppermute | solution.py:415
  63.4 14.4 %collective-permute-start.13 = (f32[1,4096]{1,0:T(1,128)S(1)}, f32[1,4096]{1,0:T(1,128)S(1)}, u32[]{:S(2)}, u32[]{:S(2)}) collective-permute-start(f32[1,4096]{1,0:T(1,128)S(1)} %log_add_fusion.4), channel_id=1, source_target_pairs={{0,16},{2,18},{4,20},{6,22},{8,24},{10,26},{12,28},{14,30},{16,0},... | collective-permute-start | bytes 49160 | tf_op jit(solution)/shard_map/ppermute | solution.py:415
  64.2 13.6 %collective-permute-start.14 = (f32[1,4096]{1,0:T(1,128)S(1)}, f32[1,4096]{1,0:T(1,128)S(1)}, u32[]{:S(2)}, u32[]{:S(2)}) collective-permute-start(f32[1,4096]{1,0:T(1,128)S(1)} %log_add_fusion.4), channel_id=1, source_target_pairs={{0,24},{2,26},{4,28},{6,30},{8,16},{10,18},{12,20},{14,22},{16,8},... | collective-permute-start | bytes 49160 | tf_op jit(solution)/shard_map/ppermute | solution.py:415
  81.5 9.4 %collective-permute-start.18 = (f32[1,4096]{1,0:T(1,128)S(1)}, f32[1,4096]{1,0:T(1,128)S(1)}, u32[]{:S(2)}, u32[]{:S(2)}) collective-permute-start(f32[1,4096]{1,0:T(1,128)S(1)} %get-tuple-element.51), channel_id=1, source_target_pairs={{0,1},{1,0},{2,3},{3,2},{4,5},{5,4},{6,7},{7,6},{8,9},{9,8},{10,11... | collective-permute-start | bytes 49160 | tf_op jit(solution)/shard_map/ppermute | solution.py:389
  93.2 6.1 %collective-permute-start.21 = (f32[2,4096]{1,0:T(2,128)S(1)}, f32[2,4096]{1,0:T(2,128)S(1)}, u32[]{:S(2)}, u32[]{:S(2)}) collective-permute-start(f32[2,4096]{1,0:T(2,128)S(1)} %pad_maximum_fusion.6), channel_id=1, source_target_pairs={{0,16},{2,18},{4,20},{6,22},{8,24},{10,26},{12,28},{14,30},{16,0},... | collective-permute-start | bytes 98312 | tf_op jit(solution)/shard_map/ppermute | solution.py:415
  116.4 13.6 %collective-permute-start.27 = (f32[1,4096]{1,0:T(1,128)S(1)}, f32[1,4096]{1,0:T(1,128)S(1)}, u32[]{:S(2)}, u32[]{:S(2)}) collective-permute-start(f32[1,4096]{1,0:T(1,128)S(1)} %add.112), channel_id=1, source_target_pairs={{0,8},{2,10},{4,12},{6,14},{8,0},{10,2},{12,4},{14,6},{16,24},{18,... | collective-permute-start | bytes 49160 | tf_op jit(solution)/shard_map/ppermute | solution.py:415
  116.5 13.5 %collective-permute-start.28 = (f32[1,4096]{1,0:T(1,128)S(1)}, f32[1,4096]{1,0:T(1,128)S(1)}, u32[]{:S(2)}, u32[]{:S(2)}) collective-permute-start(f32[1,4096]{1,0:T(1,128)S(1)} %add.112), channel_id=1, source_target_pairs={{0,16},{2,18},{4,20},{6,22},{8,24},{10,26},{12,28},{14,30},{16,0},... | collective-permute-start | bytes 49160 | tf_op jit(solution)/shard_map/ppermute | solution.py:415
  118.5 11.5 %collective-permute-start.29 = (f32[1,4096]{1,0:T(1,128)S(1)}, f32[1,4096]{1,0:T(1,128)S(1)}, u32[]{:S(2)}, u32[]{:S(2)}) collective-permute-start(f32[1,4096]{1,0:T(1,128)S(1)} %add.112), channel_id=1, source_target_pairs={{0,24},{2,26},{4,28},{6,30},{8,16},{10,18},{12,20},{14,22},{16,8},... | collective-permute-start | bytes 49160 | tf_op jit(solution)/shard_map/ppermute | solution.py:415
  143.9 6.4 %collective-permute-start.36 = (f32[1,6144]{1,0:T(1,128)S(1)}, f32[1,6144]{1,0:T(1,128)S(1)}, u32[]{:S(2)}, u32[]{:S(2)}) collective-permute-start(f32[1,6144]{1,0:T(1,128)S(1)} %pad_maximum_fusion.8), channel_id=1, source_target_pairs={{0,24},{2,26},{4,28},{6,30},{8,16},{10,18},{12,20},{14,22},{16,8},... | collective-permute-start | bytes 73736 | tf_op jit(solution)/shard_map/ppermute | solution.py:415
  145.6 6.5 %collective-permute-start.34 = (f32[1,6144]{1,0:T(1,128)S(1)}, f32[1,6144]{1,0:T(1,128)S(1)}, u32[]{:S(2)}, u32[]{:S(2)}) collective-permute-start(f32[1,6144]{1,0:T(1,128)S(1)} %pad_maximum_fusion.8), channel_id=1, source_target_pairs={{0,8},{2,10},{4,12},{6,14},{8,0},{10,2},{12,4},{14,6},{16,24},{18,... | collective-permute-start | bytes 73736 | tf_op jit(solution)/shard_map/ppermute | solution.py:415
  145.6 6.5 %collective-permute-start.35 = (f32[1,6144]{1,0:T(1,128)S(1)}, f32[1,6144]{1,0:T(1,128)S(1)}, u32[]{:S(2)}, u32[]{:S(2)}) collective-permute-start(f32[1,6144]{1,0:T(1,128)S(1)} %pad_maximum_fusion.8), channel_id=1, source_target_pairs={{0,16},{2,18},{4,20},{6,22},{8,24},{10,26},{12,28},{14,30},{16,0},... | collective-permute-start | bytes 73736 | tf_op jit(solution)/shard_map/ppermute | solution.py:415
  165.2 19.4 %all-to-all-start.1 = ((bf16[16,8,2048]{2,1,0:T(8,128)(2,1)}), bf16[16,8,2048]{2,1,0:T(8,128)(2,1)S(1)}, u32[]{:S(2)}, u32[]{:S(2)}) async-start(bf16[16,8,2048]{2,1,0:T(8,128)(2,1)} %bitcast.42), calls=%async_computation.1 | async-start | bytes 1048576 | tf_op jit(solution)/shard_map/all_to_all | solution.py:525
  (25 other events, 120.9 us)
Sparse Core Ops, SparseCore 0:
  41.6 115.7 all-gather.1
where the time goes:
time: 195 us
  Pallas kernels  70.6 us (36%)
  starting transfers between devices  59 us (30%)
  waiting for transfers between devices  44.8 us (23%)
  between operations  14.5 us (7%)
  other arithmetic  3.65 us (2%)
  local copies, waits for them, and re-layouts  2.36 us (1%)
    ppermute x33, starting transfers between devices, swap(): return lax.ppermute(v, 'dp', [(a, a ^ mask) for a in range(size)])  45.4 us
    ppermute x33, waiting for transfers between devices, swap(): return lax.ppermute(v, 'dp', [(a, a ^ mask) for a in range(size)])  39.3 us
    pallas_call x2, Pallas kernels, exp_rows(): pl.pallas_call(functools.partial(exp_kernel, rb, 128, resident), in_specs...  22 us
    pallas_call x3, Pallas kernels, sweep(): pl.pallas_call(functools.partial(sweep_kernel, first, float(n_all), float...  18.9 us
    pallas_call x1, Pallas kernels, logit_grads(): pl.pallas_call(functools.partial(logit_kernel, float(protos_all), share,...  14.8 us
    pallas_call x1, Pallas kernels, soft_part(): pl.pallas_call(soft_kernel, grid=(width // kb,), in_specs=[pl.BlockSpec((...  9.11 us
    all_to_all x1, starting transfers between devices, shards(): own = lax.all_to_all(prototypes, 'dp', 1, 0, tiled=True)  8.32 us
    pallas_call x1, Pallas kernels, proto_grad_columns(): pl.pallas_call(functools.partial(grad_kernel, scale), in_specs=[WHOLE] *...  5.81 us
  transfers between devices with their start and end apart: 44, of which 29 were waited for; matrix products, arithmetic and copies ran while one was open for 2% of the time, Pallas kernels for 36%

commit v1 on v0

--- a/solution.py
+++ b/solution.py
@@ -472,12 +472,15 @@
     protos_all = prototypes.shape[1] * lax.axis_size("proto")
     width = prototypes.shape[1] // dp
 
-    own = lax.all_to_all(prototypes, "dp", 1, 0, tiled=True)
     crops = jnp.stack([own_share(teacher), own_share(student)])[None]
     rounds = dp_rounds()
-    for masks in rounds[:-1]:
+    got = from_partners(crops, rounds[0])
+    mine, got[1] = lax.optimization_barrier((prototypes, got[1]))
+    own = lax.all_to_all(mine, "dp", 1, 0, tiled=True)
+    crops = jnp.stack(got, axis=1).reshape((-1,) + crops.shape[1:])
+    for masks in rounds[1:-1]:
         crops = gather_round(crops, masks)
-    own, crops, prototypes = lax.optimization_barrier((own, crops, prototypes))
+    own, prototypes = lax.optimization_barrier((own, prototypes))
     gathered = lax.all_gather(prototypes, "dp", axis=0, tiled=True)
     teacher_all, student_all = [
         both_shares(in_dp_order(gather_round(crops[:, i], rounds[-1]))).reshape(n, depth)

time: 195 us -> 190 us (0.974)
  waiting for transfers between devices: 44.8 us -> 39.9 us
    ppermute x33, waiting for transfers between devices: 39.3 us -> 32.4 us  [swap(): return lax.ppermute(v, 'dp', [(a, a ^ mask) for a in range(size)])]
  transfers between devices with their start and end apart: 44 -> 44, of which waited for: 29 -> 27; matrix products, arithmetic and copies ran while one was open for 2% -> 2% of each run, Pallas kernels for 36% -> 37%
where the time goes in v1:
time: 190 us; the launch traced here: 189 us
  Pallas kernels  70.6 us (37%)
  starting transfers between devices  58.4 us (31%)
  waiting for transfers between devices  39.9 us (21%)
  between operations  14.5 us (8%)
  other arithmetic  3.67 us (2%)
  local copies, waits for them, and re-layouts  2.35 us (1%)
    ppermute x33, starting transfers between devices, swap(): return lax.ppermute(v, 'dp', [(a, a ^ mask) for a in range(size)])  46.7 us
    ppermute x33, waiting for transfers between devices, swap(): return lax.ppermute(v, 'dp', [(a, a ^ mask) for a in range(size)])  32.4 us
    pallas_call x2, Pallas kernels, exp_rows(): pl.pallas_call(functools.partial(exp_kernel, rb, 128, resident), in_specs...  21.9 us
    pallas_call x3, Pallas kernels, sweep(): pl.pallas_call(functools.partial(sweep_kernel, first, float(n_all), float...  18.9 us
    pallas_call x1, Pallas kernels, logit_grads(): pl.pallas_call(functools.partial(logit_kernel, float(protos_all), share,...  14.8 us
    pallas_call x1, Pallas kernels, soft_part(): pl.pallas_call(soft_kernel, grid=(width // kb,), in_specs=[pl.BlockSpec((...  9.13 us
    all_to_all x1, starting transfers between devices, shards(): own = lax.all_to_all(mine, 'dp', 1, 0, tiled=True)  7.6 us
    pallas_call x1, Pallas kernels, proto_grad_columns(): pl.pallas_call(functools.partial(grad_kernel, scale), in_specs=[WHOLE] *...  5.81 us
  transfers between devices with their start and end apart: 44, of which 27 were waited for; matrix products, arithmetic and copies ran while one was open for 2% of the time, Pallas kernels for 37%

profile of v1, /device:TPU:0, one launch (start us, length us, event | category | flops | bytes accessed | tf_op | source)
XLA Modules:
  0.0 189.4 jit_solution(6803561559348141679)
XLA Ops:
  8.0 3.1 %collective-permute-start = (bf16[1,2,128,128]{3,2,1,0:T(8,128)(2,1)S(1)}, bf16[1,2,128,128]{3,2,1,0:T(8,128)(2,1)S(1)}, u32[]{:S(2)}, u32[]{:S(2)}) collective-permute-start(bf16[1,2,128,128]{3,2,1,0:T(8,128)(2,1)S(1)} %get-tuple-element.80), channel_id=1, source_target_pairs={{0,8},{2,10},{4,12},{6,14},{8,0},{10,2},{12,4},{14,6},{16,24},{18,... | collective-permute-start | bytes 196616 | tf_op jit(solution)/shard_map/ppermute | solution.py:415
  11.1 2.6 %collective-permute-start.1 = (bf16[1,2,128,128]{3,2,1,0:T(8,128)(2,1)S(1)}, bf16[1,2,128,128]{3,2,1,0:T(8,128)(2,1)S(1)}, u32[]{:S(2)}, u32[]{:S(2)}) collective-permute-start(bf16[1,2,128,128]{3,2,1,0:T(8,128)(2,1)S(1)} %get-tuple-element.80), channel_id=1, source_target_pairs={{0,16},{2,18},{4,20},{6,22},{8,24},{10,26},{12,28},{14,30},{16,0},... | collective-permute-start | bytes 196616 | tf_op jit(solution)/shard_map/ppermute | solution.py:415
  13.7 7.6 %all-to-all-start = ((bf16[8,16,2048]{2,0,1:T(8,128)(2,1)}), bf16[8,16,2048]{2,0,1:T(8,128)(2,1)S(1)}, u32[]{:S(2)}, u32[]{:S(2)}) async-start(bf16[8,16,2048]{2,0,1:T(8,128)(2,1)} %bitcast.79), calls=%async_computation | async-start | bytes 1048576 | tf_op jit(solution)/shard_map/all_to_all | solution.py:479
  28.4 3.8 %collective-permute-done.3 = bf16[4,128,128]{2,1,0:T(8,128)(2,1)S(1)} collective-permute-done((bf16[4,128,128]{2,1,0:T(8,128)(2,1)S(1)}, bf16[4,128,128]{2,1,0:T(8,128)(2,1)S(1)}, u32[]{:S(2)}, u32[]{:S(2)}) %collective-permute-start.3) | collective-permute-done | bytes 131104 | tf_op jit(solution)/shard_map/ppermute | solution.py:415
  34.1 2.5 %collective-permute-done.5 = bf16[4,128,128]{2,1,0:T(8,128)(2,1)S(1)} collective-permute-done((bf16[4,128,128]{2,1,0:T(8,128)(2,1)S(1)}, bf16[4,128,128]{2,1,0:T(8,128)(2,1)S(1)}, u32[]{:S(2)}, u32[]{:S(2)}) %collective-permute-start.5) | collective-permute-done | bytes 131104 | tf_op jit(solution)/shard_map/ppermute | solution.py:415
  42.8 10.1 %exp_rows.2 = (bf16[2048,4096]{1,0:T(8,128)(2,1)S(1)}, f32[1,4096]{1,0:T(1,128)S(1)}, f32[1,4096]{1,0:T(1,128)S(1)}) custom-call(bf16[128,2048]{1,0:T(8,128)(2,1)S(1)} %bitcast.74, bf16[4096,128]{1,0:T(8,128)(2,1)S(1)} %bitcast.73), custom_call_target="tpu_custom_call" | custom-call | flops 2147483648 | bytes 16777216 | tf_op jit(solution)/shard_map/exp_rows/pallas_call | solution.py:125
  55.5 2.4 %collective-permute-start.13 = (f32[1,4096]{1,0:T(1,128)S(1)}, f32[1,4096]{1,0:T(1,128)S(1)}, u32[]{:S(2)}, u32[]{:S(2)}) collective-permute-start(f32[1,4096]{1,0:T(1,128)S(1)} %log_add_fusion.4), channel_id=1, source_target_pairs={{0,16},{2,18},{4,20},{6,22},{8,24},{10,26},{12,28},{14,30},{16,0},... | collective-permute-start | bytes 49160 | tf_op jit(solution)/shard_map/ppermute | solution.py:415
  58.7 11.9 %exp_rows.3 = (bf16[2048,4096]{1,0:T(8,128)(2,1)}, f32[1,4096]{1,0:T(1,128)S(1)}, f32[1,4096]{1,0:T(1,128)S(1)}) custom-call(bf16[128,2048]{1,0:T(8,128)(2,1)S(1)} %bitcast.75, bf16[4096,128]{1,0:T(8,128)(2,1)S(1)} %bitcast.70), custom_call_target="tpu_custom_call" | custom-call | flops 2147483648 | bytes 16777216 | tf_op jit(solution)/shard_map/exp_rows/pallas_call | solution.py:125
  72.2 2.0 %collective-permute-start.17 = (f32[1,4096]{1,0:T(1,128)S(1)}, f32[1,4096]{1,0:T(1,128)S(1)}, u32[]{:S(2)}, u32[]{:S(2)}) collective-permute-start(f32[1,4096]{1,0:T(1,128)S(1)} %log_add_fusion.3.refs_0_), channel_id=1, source_target_pairs={{0,6},{2,4},{4,2},{6,0},{8,14},{10,12},{12,10},{14,8},{16,22},{18,... | collective-permute-start | bytes 49160 | tf_op jit(solution)/shard_map/ppermute | solution.py:415
  77.2 6.4 %sweep.3 = (f32[1,4096]{1,0:T(1,128)S(1)}, f32[1,2048]{1,0:T(1,128)}, f32[2,4096]{1,0:T(2,128)S(1)}) custom-call(bf16[2048,4096]{1,0:T(8,128)(2,1)S(1)} %get-tuple-element.40.x, f32[1,4096]{1,0:T(1,128)S(1)} %get-tuple-element.41.lead, f32[1,4096]{1,0:T(1,128)S(1)} %log_add_fusion.3.refs_0_, f32[1,4096]{1,0:T(1,128)S(1)} %collective-permute-done.15.refs_1_, ...), custom_call_target="tpu_custom_call" | custom-call | flops 33554432 | bytes 16777216 | tf_op jit(solution)/shard_map/sweep/pallas_call | solution.py:195
  85.5 2.9 %collective-permute-start.21 = (f32[2,4096]{1,0:T(2,128)S(1)}, f32[2,4096]{1,0:T(2,128)S(1)}, u32[]{:S(2)}, u32[]{:S(2)}) collective-permute-start(f32[2,4096]{1,0:T(2,128)S(1)} %pad_maximum_fusion.6), channel_id=1, source_target_pairs={{0,16},{2,18},{4,20},{6,22},{8,24},{10,26},{12,28},{14,30},{16,0},... | collective-permute-start | bytes 98312 | tf_op jit(solution)/shard_map/ppermute | solution.py:415
  90.6 2.8 %collective-permute-done.21 = f32[2,4096]{1,0:T(2,128)S(1)} collective-permute-done((f32[2,4096]{1,0:T(2,128)S(1)}, f32[2,4096]{1,0:T(2,128)S(1)}, u32[]{:S(2)}, u32[]{:S(2)}) %collective-permute-start.21) | collective-permute-done | bytes 32800 | tf_op jit(solution)/shard_map/ppermute | solution.py:415
  100.2 2.4 %collective-permute-done.25 = f32[2,4096]{1,0:T(2,128)S(1)} collective-permute-done((f32[2,4096]{1,0:T(2,128)S(1)}, f32[2,4096]{1,0:T(2,128)S(1)}, u32[]{:S(2)}, u32[]{:S(2)}) %collective-permute-start.25) | collective-permute-done | bytes 32800 | tf_op jit(solution)/shard_map/ppermute | solution.py:415
  102.7 6.2 %sweep.4 = (f32[1,4096]{1,0:T(1,128)S(1)}, f32[1,2048]{1,0:T(1,128)}, f32[2,4096]{1,0:T(2,128)}) custom-call(bf16[2048,4096]{1,0:T(8,128)(2,1)S(1)} %get-tuple-element.40.x, f32[1,4096]{1,0:T(1,128)S(1)} %get-tuple-element.85.lead.factor, f32[1,4096]{1,0:T(1,128)S(1)} %get-tuple-element.77.refs_0_, f32[1,4096]{1,0:T(1,128)S(1)} %get-tuple-element.84.refs_1_, ...), custom_call_target="tpu_custom_call" | custom-call | flops 33554432 | bytes 16777216 | tf_op jit(solution)/shard_map/sweep/pallas_call | solution.py:195
  110.1 2.2 %collective-permute-start.27 = (f32[1,4096]{1,0:T(1,128)S(1)}, f32[1,4096]{1,0:T(1,128)S(1)}, u32[]{:S(2)}, u32[]{:S(2)}) collective-permute-start(f32[1,4096]{1,0:T(1,128)S(1)} %add.112), channel_id=1, source_target_pairs={{0,8},{2,10},{4,12},{6,14},{8,0},{10,2},{12,4},{14,6},{16,24},{18,... | collective-permute-start | bytes 49160 | tf_op jit(solution)/shard_map/ppermute | solution.py:415
  114.7 9.1 %soft_part.1.soft = f32[2048,128]{1,0:T(8,128)S(1)} custom-call(bf16[2048,4096]{1,0:T(8,128)(2,1)} %get-tuple-element.58.x, f32[1,4096]{1,0:T(1,128)S(1)} %get-tuple-element.59.peak, f32[1,4096]{1,0:T(1,128)S(1)} %get-tuple-element.82.lse.glob_s, bf16[4096,128]{1,0:T(8,128)(2,1)S(1)} %bitcast.71), custom_call_target="tpu_custom_call" | custom-call | flops 2147483648 | bytes 16777216 | tf_op jit(solution)/shard_map/soft_part/pallas_call | solution.py:235
  125.2 2.2 %collective-permute-start.32 = (f32[1,4096]{1,0:T(1,128)S(1)}, f32[1,4096]{1,0:T(1,128)S(1)}, u32[]{:S(2)}, u32[]{:S(2)}) collective-permute-start(f32[1,4096]{1,0:T(1,128)S(1)} %add_add_fusion.refs_0_), channel_id=1, source_target_pairs={{0,6},{2,4},{4,2},{6,0},{8,14},{10,12},{12,10},{14,8},{16,22},{18,... | collective-permute-start | bytes 49160 | tf_op jit(solution)/shard_map/ppermute | solution.py:415
  130.2 6.4 %sweep.5 = (f32[1,4096]{1,0:T(1,128)S(1)}, f32[1,2048]{1,0:T(1,128)S(1)}, f32[2,4096]{1,0:T(2,128)}) custom-call(bf16[2048,4096]{1,0:T(8,128)(2,1)S(1)} %get-tuple-element.40.x, f32[1,4096]{1,0:T(1,128)S(1)} %get-tuple-element.85.lead.factor, f32[1,4096]{1,0:T(1,128)S(1)} %add_add_fusion.refs_0_, f32[1,4096]{1,0:T(1,128)S(1)} %collective-permute-done.30.refs_1_, ...), custom_call_target="tpu_custom_call" | custom-call | flops 33554432 | bytes 16777216 | tf_op jit(solution)/shard_map/sweep/pallas_call | solution.py:195
  137.8 2.5 %collective-permute-start.36 = (f32[1,6144]{1,0:T(1,128)S(1)}, f32[1,6144]{1,0:T(1,128)S(1)}, u32[]{:S(2)}, u32[]{:S(2)}) collective-permute-start(f32[1,6144]{1,0:T(1,128)S(1)} %pad_maximum_fusion.8), channel_id=1, source_target_pairs={{0,24},{2,26},{4,28},{6,30},{8,16},{10,18},{12,20},{14,22},{16,8},... | collective-permute-start | bytes 73736 | tf_op jit(solution)/shard_map/ppermute | solution.py:415
  142.2 2.0 %collective-permute-done.36 = f32[1,6144]{1,0:T(1,128)S(1)} collective-permute-done((f32[1,6144]{1,0:T(1,128)S(1)}, f32[1,6144]{1,0:T(1,128)S(1)}, u32[]{:S(2)}, u32[]{:S(2)}) %collective-permute-start.36) | collective-permute-done | bytes 24608 | tf_op jit(solution)/shard_map/ppermute | solution.py:415
  144.2 3.3 %collective-permute-done.35 = f32[1,6144]{1,0:T(1,128)S(1)} collective-permute-done((f32[1,6144]{1,0:T(1,128)S(1)}, f32[1,6144]{1,0:T(1,128)S(1)}, u32[]{:S(2)}, u32[]{:S(2)}) %collective-permute-start.35) | collective-permute-done | bytes 24608 | tf_op jit(solution)/shard_map/ppermute | solution.py:415
  154.8 5.8 %proto_grad.1 = bf16[128,2048]{1,0:T(8,128)(2,1)} custom-call(bf16[2048,4096]{1,0:T(8,128)(2,1)S(1)} %get-tuple-element.40.x, f32[1,4096]{1,0:T(1,128)S(1)} %get-tuple-element.85.lead.factor, bf16[4096,128]{1,0:T(8,128)(2,1)S(1)} %bitcast.72, f32[2048,128]{1,0:T(8,128)S(1)} %soft_part.1.soft, f32[1,2048]{1,0:T(1,128)S(1)} %get-tuple-element.65.col, ...), custom_call_target="tpu_custom_call" | custom-call | flops 2147483648 | bytes 16777216 | tf_op jit(solution)/shard_map/proto_grad/pallas_call | solution.py:271
  160.6 3.6 %all-to-all-start.1 = ((bf16[16,8,2048]{2,1,0:T(8,128)(2,1)}), bf16[16,8,2048]{2,1,0:T(8,128)(2,1)S(1)}, u32[]{:S(2)}, u32[]{:S(2)}) async-start(bf16[16,8,2048]{2,1,0:T(8,128)(2,1)} %bitcast.42), calls=%async_computation.1 | async-start | bytes 1048576 | tf_op jit(solution)/shard_map/all_to_all | solution.py:528
  164.3 14.8 %logit_grads.1 = (bf16[256,32768]{1,0:T(8,128)(2,1)}, f32[1,256]{1,0:T(1,128)}) custom-call(bf16[128,32768]{1,0:T(8,128)(2,1)} %all-gather.2.cloned.1.call-done.protos, bf16[256,128]{1,0:T(8,128)(2,1)} %teacher.1, bf16[256,128]{1,0:T(8,128)(2,1)} %student.1, f32[1,4096]{1,0:T(1,128)} %get-tuple-element.86.glob_t, f32[1,4096]{1,0:T(1,128)} %copy-done.1, ...), custom_call_target="tpu_custom_call" | custom-call | flops 4294967296 | bytes 25165824 | tf_op jit(solution)/shard_map/logit_grads/pallas_call | solution.py:362
  (123 shorter events, 56.5 us)
Async XLA Ops:
  11.1 10.2 %collective-permute-start.1 = (bf16[1,2,128,128]{3,2,1,0:T(8,128)(2,1)S(1)}, bf16[1,2,128,128]{3,2,1,0:T(8,128)(2,1)S(1)}, u32[]{:S(2)}, u32[]{:S(2)}) collective-permute-start(bf16[1,2,128,128]{3,2,1,0:T(8,128)(2,1)S(1)} %get-tuple-element.80), channel_id=1, source_target_pairs={{0,16},{2,18},{4,20},{6,22},{8,24},{10,26},{12,28},{14,30},{16,0},... | collective-permute-start | bytes 196616 | tf_op jit(solution)/shard_map/ppermute | solution.py:415
  13.6 7.7 %collective-permute-start.2 = (bf16[1,2,128,128]{3,2,1,0:T(8,128)(2,1)S(1)}, bf16[1,2,128,128]{3,2,1,0:T(8,128)(2,1)S(1)}, u32[]{:S(2)}, u32[]{:S(2)}) collective-permute-start(bf16[1,2,128,128]{3,2,1,0:T(8,128)(2,1)S(1)} %get-tuple-element.80), channel_id=1, source_target_pairs={{0,24},{2,26},{4,28},{6,30},{8,16},{10,18},{12,20},{14,22},{16,8},... | collective-permute-start | bytes 196616 | tf_op jit(solution)/shard_map/ppermute | solution.py:415
  13.7 23.4 %all-to-all-start = ((bf16[8,16,2048]{2,0,1:T(8,128)(2,1)}), bf16[8,16,2048]{2,0,1:T(8,128)(2,1)S(1)}, u32[]{:S(2)}, u32[]{:S(2)}) async-start(bf16[8,16,2048]{2,0,1:T(8,128)(2,1)} %bitcast.79), calls=%async_computation | async-start | bytes 1048576 | tf_op jit(solution)/shard_map/all_to_all | solution.py:479
  21.3 143.0 %all-gather.2.cloned.1.call-start = ((), (), s32[]{:S(2)}) async-start(), calls=%async_computation.2 | async-start | bytes 8912896 | tf_op jit(solution)/shard_map/all_gather | solution.py:484
  21.5 10.7 %collective-permute-start.3 = (bf16[4,128,128]{2,1,0:T(8,128)(2,1)S(1)}, bf16[4,128,128]{2,1,0:T(8,128)(2,1)S(1)}, u32[]{:S(2)}, u32[]{:S(2)}) collective-permute-start(bf16[4,128,128]{2,1,0:T(8,128)(2,1)S(1)} %get-tuple-element.74), channel_id=1, source_target_pairs={{0,2},{2,0},{4,6},{6,4},{8,10},{10,8},{12,14},{14,12},{16,18},{18,... | collective-permute-start | bytes 393224 | tf_op jit(solution)/shard_map/ppermute | solution.py:415
  23.5 10.6 %collective-permute-start.4 = (bf16[4,128,128]{2,1,0:T(8,128)(2,1)S(1)}, bf16[4,128,128]{2,1,0:T(8,128)(2,1)S(1)}, u32[]{:S(2)}, u32[]{:S(2)}) collective-permute-start(bf16[4,128,128]{2,1,0:T(8,128)(2,1)S(1)} %get-tuple-element.74), channel_id=1, source_target_pairs={{0,4},{2,6},{4,0},{6,2},{8,12},{10,14},{12,8},{14,10},{16,20},{18,... | collective-permute-start | bytes 393224 | tf_op jit(solution)/shard_map/ppermute | solution.py:415
  24.9 11.7 %collective-permute-start.5 = (bf16[4,128,128]{2,1,0:T(8,128)(2,1)S(1)}, bf16[4,128,128]{2,1,0:T(8,128)(2,1)S(1)}, u32[]{:S(2)}, u32[]{:S(2)}) collective-permute-start(bf16[4,128,128]{2,1,0:T(8,128)(2,1)S(1)} %get-tuple-element.74), channel_id=1, source_target_pairs={{0,6},{2,4},{4,2},{6,0},{8,14},{10,12},{12,10},{14,8},{16,22},{18,... | collective-permute-start | bytes 393224 | tf_op jit(solution)/shard_map/ppermute | solution.py:415
  25.0 12.8 %collective-permute-start.8 = (bf16[4,128,128]{2,1,0:T(8,128)(2,1)S(1)}, bf16[4,128,128]{2,1,0:T(8,128)(2,1)S(1)}, u32[]{:S(2)}, u32[]{:S(2)}) collective-permute-start(bf16[4,128,128]{2,1,0:T(8,128)(2,1)S(1)} %get-tuple-element.75), channel_id=1, source_target_pairs={{0,2},{2,0},{4,6},{6,4},{8,10},{10,8},{12,14},{14,12},{16,18},{18,... | collective-permute-start | bytes 393224 | tf_op jit(solution)/shard_map/ppermute | solution.py:415
  27.0 11.2 %collective-permute-start.9 = (bf16[4,128,128]{2,1,0:T(8,128)(2,1)S(1)}, bf16[4,128,128]{2,1,0:T(8,128)(2,1)S(1)}, u32[]{:S(2)}, u32[]{:S(2)}) collective-permute-start(bf16[4,128,128]{2,1,0:T(8,128)(2,1)S(1)} %get-tuple-element.75), channel_id=1, source_target_pairs={{0,4},{2,6},{4,0},{6,2},{8,12},{10,14},{12,8},{14,10},{16,20},{18,... | collective-permute-start | bytes 393224 | tf_op jit(solution)/shard_map/ppermute | solution.py:415
  32.2 7.9 %collective-permute-start.10 = (bf16[4,128,128]{2,1,0:T(8,128)(2,1)S(1)}, bf16[4,128,128]{2,1,0:T(8,128)(2,1)S(1)}, u32[]{:S(2)}, u32[]{:S(2)}) collective-permute-start(bf16[4,128,128]{2,1,0:T(8,128)(2,1)S(1)} %get-tuple-element.75), channel_id=1, source_target_pairs={{0,6},{2,4},{4,2},{6,0},{8,14},{10,12},{12,10},{14,8},{16,22},{18,... | collective-permute-start | bytes 393224 | tf_op jit(solution)/shard_map/ppermute | solution.py:415
  54.2 16.4 %collective-permute-start.12 = (f32[1,4096]{1,0:T(1,128)S(1)}, f32[1,4096]{1,0:T(1,128)S(1)}, u32[]{:S(2)}, u32[]{:S(2)}) collective-permute-start(f32[1,4096]{1,0:T(1,128)S(1)} %log_add_fusion.4), channel_id=1, source_target_pairs={{0,8},{2,10},{4,12},{6,14},{8,0},{10,2},{12,4},{14,6},{16,24},{18,... | collective-permute-start | bytes 49160 | tf_op jit(solution)/shard_map/ppermute | solution.py:415
  55.5 15.0 %collective-permute-start.13 = (f32[1,4096]{1,0:T(1,128)S(1)}, f32[1,4096]{1,0:T(1,128)S(1)}, u32[]{:S(2)}, u32[]{:S(2)}) collective-permute-start(f32[1,4096]{1,0:T(1,128)S(1)} %log_add_fusion.4), channel_id=1, source_target_pairs={{0,16},{2,18},{4,20},{6,22},{8,24},{10,26},{12,28},{14,30},{16,0},... | collective-permute-start | bytes 49160 | tf_op jit(solution)/shard_map/ppermute | solution.py:415
  57.9 12.7 %collective-permute-start.14 = (f32[1,4096]{1,0:T(1,128)S(1)}, f32[1,4096]{1,0:T(1,128)S(1)}, u32[]{:S(2)}, u32[]{:S(2)}) collective-permute-start(f32[1,4096]{1,0:T(1,128)S(1)} %log_add_fusion.4), channel_id=1, source_target_pairs={{0,24},{2,26},{4,28},{6,30},{8,16},{10,18},{12,20},{14,22},{16,8},... | collective-permute-start | bytes 49160 | tf_op jit(solution)/shard_map/ppermute | solution.py:415
  74.3 9.3 %collective-permute-start.18 = (f32[1,4096]{1,0:T(1,128)S(1)}, f32[1,4096]{1,0:T(1,128)S(1)}, u32[]{:S(2)}, u32[]{:S(2)}) collective-permute-start(f32[1,4096]{1,0:T(1,128)S(1)} %get-tuple-element.53), channel_id=1, source_target_pairs={{0,1},{1,0},{2,3},{3,2},{4,5},{5,4},{6,7},{7,6},{8,9},{9,8},{10,11... | collective-permute-start | bytes 49160 | tf_op jit(solution)/shard_map/ppermute | solution.py:389
  84.8 5.8 %collective-permute-start.20 = (f32[2,4096]{1,0:T(2,128)S(1)}, f32[2,4096]{1,0:T(2,128)S(1)}, u32[]{:S(2)}, u32[]{:S(2)}) collective-permute-start(f32[2,4096]{1,0:T(2,128)S(1)} %pad_maximum_fusion.6), channel_id=1, source_target_pairs={{0,8},{2,10},{4,12},{6,14},{8,0},{10,2},{12,4},{14,6},{16,24},{18,... | collective-permute-start | bytes 98312 | tf_op jit(solution)/shard_map/ppermute | solution.py:415
  85.5 8.0 %collective-permute-start.21 = (f32[2,4096]{1,0:T(2,128)S(1)}, f32[2,4096]{1,0:T(2,128)S(1)}, u32[]{:S(2)}, u32[]{:S(2)}) collective-permute-start(f32[2,4096]{1,0:T(2,128)S(1)} %pad_maximum_fusion.6), channel_id=1, source_target_pairs={{0,16},{2,18},{4,20},{6,22},{8,24},{10,26},{12,28},{14,30},{16,0},... | collective-permute-start | bytes 98312 | tf_op jit(solution)/shard_map/ppermute | solution.py:415
  88.4 6.4 %collective-permute-start.22 = (f32[2,4096]{1,0:T(2,128)S(1)}, f32[2,4096]{1,0:T(2,128)S(1)}, u32[]{:S(2)}, u32[]{:S(2)}) collective-permute-start(f32[2,4096]{1,0:T(2,128)S(1)} %pad_maximum_fusion.6), channel_id=1, source_target_pairs={{0,24},{2,26},{4,28},{6,30},{8,16},{10,18},{12,20},{14,22},{16,8},... | collective-permute-start | bytes 98312 | tf_op jit(solution)/shard_map/ppermute | solution.py:415
  110.1 13.8 %collective-permute-start.27 = (f32[1,4096]{1,0:T(1,128)S(1)}, f32[1,4096]{1,0:T(1,128)S(1)}, u32[]{:S(2)}, u32[]{:S(2)}) collective-permute-start(f32[1,4096]{1,0:T(1,128)S(1)} %add.112), channel_id=1, source_target_pairs={{0,8},{2,10},{4,12},{6,14},{8,0},{10,2},{12,4},{14,6},{16,24},{18,... | collective-permute-start | bytes 49160 | tf_op jit(solution)/shard_map/ppermute | solution.py:415
  112.3 11.6 %collective-permute-start.28 = (f32[1,4096]{1,0:T(1,128)S(1)}, f32[1,4096]{1,0:T(1,128)S(1)}, u32[]{:S(2)}, u32[]{:S(2)}) collective-permute-start(f32[1,4096]{1,0:T(1,128)S(1)} %add.112), channel_id=1, source_target_pairs={{0,16},{2,18},{4,20},{6,22},{8,24},{10,26},{12,28},{14,30},{16,0},... | collective-permute-start | bytes 49160 | tf_op jit(solution)/shard_map/ppermute | solution.py:415
  113.0 10.9 %collective-permute-start.29 = (f32[1,4096]{1,0:T(1,128)S(1)}, f32[1,4096]{1,0:T(1,128)S(1)}, u32[]{:S(2)}, u32[]{:S(2)}) collective-permute-start(f32[1,4096]{1,0:T(1,128)S(1)} %add.112), channel_id=1, source_target_pairs={{0,24},{2,26},{4,28},{6,30},{8,16},{10,18},{12,20},{14,22},{16,8},... | collective-permute-start | bytes 49160 | tf_op jit(solution)/shard_map/ppermute | solution.py:415
  137.8 6.4 %collective-permute-start.36 = (f32[1,6144]{1,0:T(1,128)S(1)}, f32[1,6144]{1,0:T(1,128)S(1)}, u32[]{:S(2)}, u32[]{:S(2)}) collective-permute-start(f32[1,6144]{1,0:T(1,128)S(1)} %pad_maximum_fusion.8), channel_id=1, source_target_pairs={{0,24},{2,26},{4,28},{6,30},{8,16},{10,18},{12,20},{14,22},{16,8},... | collective-permute-start | bytes 73736 | tf_op jit(solution)/shard_map/ppermute | solution.py:415
  140.3 7.3 %collective-permute-start.34 = (f32[1,6144]{1,0:T(1,128)S(1)}, f32[1,6144]{1,0:T(1,128)S(1)}, u32[]{:S(2)}, u32[]{:S(2)}) collective-permute-start(f32[1,6144]{1,0:T(1,128)S(1)} %pad_maximum_fusion.8), channel_id=1, source_target_pairs={{0,8},{2,10},{4,12},{6,14},{8,0},{10,2},{12,4},{14,6},{16,24},{18,... | collective-permute-start | bytes 73736 | tf_op jit(solution)/shard_map/ppermute | solution.py:415
  140.4 7.2 %collective-permute-start.35 = (f32[1,6144]{1,0:T(1,128)S(1)}, f32[1,6144]{1,0:T(1,128)S(1)}, u32[]{:S(2)}, u32[]{:S(2)}) collective-permute-start(f32[1,6144]{1,0:T(1,128)S(1)} %pad_maximum_fusion.8), channel_id=1, source_target_pairs={{0,16},{2,18},{4,20},{6,22},{8,24},{10,26},{12,28},{14,30},{16,0},... | collective-permute-start | bytes 73736 | tf_op jit(solution)/shard_map/ppermute | solution.py:415
  160.6 18.5 %all-to-all-start.1 = ((bf16[16,8,2048]{2,1,0:T(8,128)(2,1)}), bf16[16,8,2048]{2,1,0:T(8,128)(2,1)S(1)}, u32[]{:S(2)}, u32[]{:S(2)}) async-start(bf16[16,8,2048]{2,1,0:T(8,128)(2,1)} %bitcast.42), calls=%async_computation.1 | async-start | bytes 1048576 | tf_op jit(solution)/shard_map/all_to_all | solution.py:528
  (25 other events, 117.3 us)
Sparse Core Ops, SparseCore 0:
  37.2 119.2 all-gather.1
